TPU v7x, 128 devices: a whole 4x4x4 slice. The times are simulated.
128 devices in a mesh: tok: 64 (over y, z_hi, x, core), head: 2 (over z_lo).
Axes of the slice: x: 4, y: 4, z: 4 (z_hi: 2, z_lo: 2; z = z_hi * 2 + z_lo), core: 2. Of those that a mesh axis runs over, the one named last changes fastest.
Arguments:
- inputs: bfloat16 [2, 32768, 2048], P(None, 'tok'), may hold values from -6 to 6
- projections: bfloat16 [3, 2048, 2048], P(None, None, 'head'), may hold values from -0.125 to 0.125
- lrate: float32 [2, 32768, 4], P(None, 'tok', 'head'), may hold values from 0.1 to 1
- fast_init: bfloat16 [4, 3, 384, 512], P('head'), may hold values from -0.25 to 0.25
- gain: float32 [2048], replicated, may hold values from 0.5 to 1.5
Outputs:
- normed: bfloat16 [2, 32768, 2048], P(None, ('tok', 'head'))
All inputs are finite; a program needn't handle non-finite values.
Results may differ from a plain program's by a relative error of at most 0.018.
Values may be sent and summed in bfloat16 or wider, within the bound.
No kernel may reach another device: no remote copies, remote signals or barrier semaphores. Data moves between devices by JAX's collectives and lax.ppermute only.
A program may use at most 128 MiB of HBM per device.

v0:
```python
import jax
import jax.numpy as jnp
from jax import lax
from jax.sharding import Mesh
from jax.sharding import PartitionSpec as P

INNER = 2
TOK = ("tok_0", "tok_1", "tok_2", "tok_3")
TOK_HEAD = ("tok_0", "tok_1", "tok_2", "tok_3", "head")


step_size = 4.0


def split_up(x, dim, devices):
    shape = x.shape
    pieces = x.reshape(*shape[:dim], devices, shape[dim] // devices, *shape[dim + 1 :])
    return jnp.moveaxis(pieces, dim, 0)


def sent_and_summed(x, axis, dim):
    devices = lax.axis_size(axis)
    pieces = lax.all_to_all(split_up(x, dim, devices), axis, 0, 0, tiled=True)
    return jnp.sum(pieces, axis=0)


def summed_rows(x, axes, dim):
    far, near = axes
    pieces = split_up(x, dim, lax.axis_size(far))
    nearer = sent_and_summed(pieces, near, dim + 1)
    arrived = lax.all_to_all(nearer, far, split_axis=0, concat_axis=0, tiled=True)
    return arrived.sum(axis=0)


def from_everyone(x, axis):
    devices = lax.axis_size(axis)
    return lax.all_to_all(jnp.broadcast_to(x[None], (devices, *x.shape)), axis, 0, 0, tiled=True)


def of_everyone(x, axis):
    everything = from_everyone(x, axis)
    return jnp.sum(everything, axis=0)


def laid_out(pieces, dim):
    pieces = jnp.moveaxis(pieces, 0, dim)
    shape = pieces.shape
    return pieces.reshape(*shape[:dim], shape[dim] * shape[dim + 1], *shape[dim + 2 :])


def gather_axes(x, axes, dim):
    far, near = axes
    initial = from_everyone(x, far)
    pieces = jnp.swapaxes(from_everyone(initial, near), 0, 1)
    return laid_out(pieces.reshape(-1, *x.shape), dim)


def mult(form, left, right):
    return jnp.einsum(form, left, right, preferred_element_type=jnp.float32)


def silu_parts(hidden):
    sigma = jax.nn.sigmoid(hidden)
    return (hidden * sigma, sigma * (1.0 + hidden * (1.0 - sigma)))


def token_gradients(weights, keys, values, rates):
    hidden = mult("htd,hfd->htf", keys, weights[:, 0])
    gated = mult("htd,hfd->htf", keys, weights[:, 1])
    act, slope = silu_parts(hidden)
    mixed = (act * gated).astype(jnp.bfloat16)
    signal = (-rates[:, :, None] * values.astype(jnp.float32)).astype(jnp.bfloat16)
    grad_second = mult("htf,htd->hfd", mixed, signal)
    back = mult("htd,hfd->htf", signal, weights[:, 2])
    grad_gate = (back * act).astype(jnp.bfloat16)
    grad_first = (back * gated * slope).astype(jnp.bfloat16)
    grad_one = mult("htf,htd->hfd", grad_first, keys)
    grad_three = mult("htf,htd->hfd", grad_gate, keys)
    return jnp.stack([grad_one, grad_three, grad_second], axis=1)


def refresh(weights, summed, frob, target):
    scale = step_size / jnp.sqrt(frob + 1e-06)
    update = weights.astype(jnp.float32) - scale[:, :, None, None] * summed
    length = jnp.sqrt(jnp.sum(update * update, axis=-1, keepdims=True) + 1e-06)
    return (update * (target / length)).astype(jnp.bfloat16)


def read_memory(weights, queries):
    hidden = mult("htd,hfd->htf", queries, weights[:, 0])
    gated = mult("htd,hfd->htf", queries, weights[:, 1])
    act, _ = silu_parts(hidden)
    mixed = (act * gated).astype(jnp.bfloat16)
    return mult("htf,hfd->htd", mixed, weights[:, 2]).astype(jnp.bfloat16)


def body(inputs, projections, lrate, fast_init, gain):
    row_count = fast_init.shape[2] // lax.axis_size(TOK)
    row_start = lax.axis_index(TOK) * row_count
    local_heads = fast_init.shape[0]
    head_width = fast_init.shape[3]
    token_count = inputs.shape[1]
    target = jnp.sqrt(jnp.sum(jnp.square(fast_init.astype(jnp.float32)), axis=-1, keepdims=True))
    target_share = lax.dynamic_slice_in_dim(target, row_start, row_count, 2)
    shaped = projections.reshape(3, projections.shape[1], local_heads, head_width)
    mapped = mult("ctd,sdhe->schte", inputs, shaped).astype(jnp.bfloat16)
    weights = fast_init
    outputs = []
    for group in range(inputs.shape[0]):
        queries, keys, values = (mapped[0, group], mapped[1, group], mapped[2, group])
        rates = lrate[group].T
        for inner in range(INNER):
            grads = token_gradients(weights, keys, values, rates)
            shares = summed_rows(grads, (("tok_0", "tok_1", "tok_2"), "tok_3"), 2)
            squares = jnp.sum(shares * shares, axis=(2, 3))
            frob = of_everyone(squares, TOK)
            former = lax.dynamic_slice_in_dim(weights, row_start, row_count, 2)
            renewed = refresh(former, shares, frob, target_share)
            weights = gather_axes(renewed, (("tok_0", "tok_1", "tok_2"), "tok_3"), 2)
        readout = read_memory(weights, queries)
        outputs.append(readout.transpose(1, 0, 2).reshape(token_count, local_heads * head_width))
    joined = jnp.stack(outputs)
    full_width = joined.shape[-1] * lax.axis_size("head")
    values_f = joined.astype(jnp.float32)
    partial_sq = jnp.sum(values_f * values_f, axis=-1)
    total_sq = of_everyone(partial_sq, "head")
    local_gain = lax.dynamic_slice_in_dim(
        gain, lax.axis_index("head") * joined.shape[-1], joined.shape[-1], 0
    )
    payload = (values_f * lax.rsqrt(total_sq[:, :, None] / full_width + 1e-06) * local_gain).astype(
        jnp.bfloat16
    )
    moved = lax.all_to_all(payload, "head", split_axis=1, concat_axis=2, tiled=True)
    return moved


def solution(mesh):
    finer = Mesh(
        mesh.devices.reshape(4, 2, 4, 2, mesh.shape["head"]),
        ("tok_0", "tok_1", "tok_2", "tok_3", "head"),
    )
    placed = (
        P(None, TOK, None),
        P(None, None, "head"),
        P(None, TOK, "head"),
        P("head", None, None, None),
        P(),
    )
    return jax.shard_map(
        body, mesh=finer, in_specs=placed, out_specs=P(None, TOK_HEAD, None), check_vma=False
    )
```

profile of v0, /device:TPU:2, one launch (start us, length us, event | category | flops | bytes accessed | tf_op | source)
XLA Modules:
  0.0 609.4 jit_solution(13451702052230497002)
XLA Ops:
  0.0 17.0 %copy.951 = bf16[3,2048,1024]{1,2,0:T(8,128)(2,1)} copy(bf16[3,2048,1024]{2,1,0:T(8,128)(2,1)} %param.6) | data formatting | bytes 25165824 | tf_op jit(solution)/shard_map/reshape | solution.py:105
  17.0 17.4 %convert_bitcast_fusion = bf16[3,2,2,512,512]{3,4,1,2,0:T(8,128)(2,1)S(1)} fusion(bf16[3,2048,2,512,1]{1,3,4,2,0:T(8,128)(2,1)} %bitcast.199, bf16[2,512,2048]{2,1,0:T(8,128)(2,1)} %param.5), kind=kOutput, calls=%fused_computation | convolution fusion | flops 12888047616 | bytes 23068672 | tf_op jit(solution)/shard_map/ctd,sdhe->schte/dot_general | solution.py:59
  46.4 3.1 copy.806
  50.5 8.6 %all_to_all.123 = f32[2,32,2,3,6,512]{5,1,4,3,2,0:T(8,128)} all-to-all(f32[2,32,2,3,6,512]{5,1,4,3,2,0:T(8,128)S(1)} %copy.807), channel_id=1, replica_groups=mesh['tok_0'=4,'tok_1'=2,'tok_2'=4,'tok_3'=2,'head'=2] {'tok_3'}, dimensions={0} | all-to-all | bytes 9437184 | tf_op jit(solution)/shard_map/all_to_all | solution.py:23
  59.1 3.1 reduce_sum.207
  62.2 3.2 copy.809
  65.4 10.9 %all-to-all-start.1 = ((f32[32,2,3,6,512]{4,1,3,2,0:T(2,128)}), f32[32,2,3,6,512]{4,1,3,2,0:T(2,128)S(1)}, u32[]{:S(2)}, u32[]{:S(2)}) async-start(f32[32,2,3,6,512]{4,1,3,2,0:T(2,128)} %copy.809), calls=%async_computation.1 | async-start | bytes 4718592 | tf_op jit(solution)/shard_map/all_to_all | solution.py:31
  78.6 32.3 %all-to-all-done.1 = f32[32,2,3,6,512]{4,1,3,2,0:T(2,128)S(1)} async-done(((f32[32,2,3,6,512]{4,1,3,2,0:T(2,128)}), f32[32,2,3,6,512]{4,1,3,2,0:T(2,128)S(1)}, u32[]{:S(2)}, u32[]{:S(2)}) %all-to-all-start.1) | async-done | bytes 2359328 | tf_op jit(solution)/shard_map/all_to_all | solution.py:31
  112.7 4.8 all-to-all-start.2
  118.4 7.6 %all-to-all-done.2 = f32[64,2,3]{2,1,0:T(2,128)S(1)} async-done(((f32[64,2,3]{2,1,0:T(2,128)}), f32[64,2,3]{2,1,0:T(2,128)S(1)}, u32[]{:S(2)}, u32[]{:S(2)}) %all-to-all-start.2) | async-done | bytes 1568 | tf_op jit(solution)/shard_map/all_to_all | solution.py:37
  127.4 24.5 %all_to_all.124 = bf16[32,2,3,6,512]{4,1,3,2,0:T(2,128)(2,1)S(1)} all-to-all(bf16[32,2,3,6,512]{4,1,3,2,0:T(2,128)(2,1)S(1)} %broadcast_in_dim.27), channel_id=1, replica_groups=mesh['tok_0'=4,'tok_1'=2,'tok_2'=4,'tok_3'=2,'head'=2] {'tok_0','tok_1',..., dimensions={0} | all-to-all | bytes 2359296 | tf_op jit(solution)/shard_map/all_to_all | solution.py:37
  154.0 5.6 all_to_all.125
  174.3 2.9 maximum_bitcast_fusion.1
  177.2 2.7 copy.832
  180.8 8.6 %all_to_all.126 = f32[2,32,2,3,6,512]{5,1,4,3,2,0:T(8,128)} all-to-all(f32[2,32,2,3,6,512]{5,1,4,3,2,0:T(8,128)S(1)} %copy.833), channel_id=1, replica_groups=mesh['tok_0'=4,'tok_1'=2,'tok_2'=4,'tok_3'=2,'head'=2] {'tok_3'}, dimensions={0} | all-to-all | bytes 9437184 | tf_op jit(solution)/shard_map/all_to_all | solution.py:23
  189.5 4.6 reduce_sum.213
  194.1 3.5 copy.835
  197.5 37.7 %all_to_all.127 = f32[32,2,3,6,512]{4,1,3,2,0:T(2,128)} all-to-all(f32[32,2,3,6,512]{4,1,3,2,0:T(2,128)S(1)} %copy.835), channel_id=1, replica_groups=mesh['tok_0'=4,'tok_1'=2,'tok_2'=4,'tok_3'=2,'head'=2] {'tok_0','tok_1',..., dimensions={0} | all-to-all | bytes 4718592 | tf_op jit(solution)/shard_map/all_to_all | solution.py:31
  237.8 13.7 %all_to_all.128 = f32[64,2,3]{2,1,0:T(2,128)S(1)} all-to-all(f32[64,2,3]{2,1,0:T(2,128)S(1)} %broadcast_in_dim.29), channel_id=1, replica_groups=mesh['tok_0'=4,'tok_1'=2,'tok_2'=4,'tok_3'=2,'head'=2] {'tok_0','tok_1',..., dimensions={0} | all-to-all | bytes 3072 | tf_op jit(solution)/shard_map/all_to_all | solution.py:37
  252.9 24.5 %all_to_all.129 = bf16[32,2,3,6,512]{4,1,3,2,0:T(2,128)(2,1)S(1)} all-to-all(bf16[32,2,3,6,512]{4,1,3,2,0:T(2,128)(2,1)S(1)} %broadcast_in_dim.30), channel_id=1, replica_groups=mesh['tok_0'=4,'tok_1'=2,'tok_2'=4,'tok_3'=2,'head'=2] {'tok_0','tok_1',..., dimensions={0} | all-to-all | bytes 2359296 | tf_op jit(solution)/shard_map/all_to_all | solution.py:37
  279.5 5.6 all_to_all.130
  290.9 3.2 copy.970
  310.2 3.1 copy.861
  314.3 8.6 %all_to_all.131 = f32[2,32,2,3,6,512]{5,1,4,3,2,0:T(8,128)} all-to-all(f32[2,32,2,3,6,512]{5,1,4,3,2,0:T(8,128)S(1)} %copy.862), channel_id=1, replica_groups=mesh['tok_0'=4,'tok_1'=2,'tok_2'=4,'tok_3'=2,'head'=2] {'tok_3'}, dimensions={0} | all-to-all | bytes 9437184 | tf_op jit(solution)/shard_map/all_to_all | solution.py:23
  322.9 3.1 reduce_sum.218
  327.8 37.0 %all_to_all.132 = f32[32,2,3,6,512]{4,1,3,2,0:T(2,128)S(1)} all-to-all(f32[32,2,3,6,512]{4,1,3,2,0:T(2,128)S(1)} %copy.864), channel_id=1, replica_groups=mesh['tok_0'=4,'tok_1'=2,'tok_2'=4,'tok_3'=2,'head'=2] {'tok_0','tok_1',..., dimensions={0} | all-to-all | bytes 4718592 | tf_op jit(solution)/shard_map/all_to_all | solution.py:31
  365.9 13.9 %all_to_all.133 = f32[64,2,3]{2,1,0:T(2,128)S(1)} all-to-all(f32[64,2,3]{2,1,0:T(2,128)S(1)} %broadcast_in_dim.32), channel_id=1, replica_groups=mesh['tok_0'=4,'tok_1'=2,'tok_2'=4,'tok_3'=2,'head'=2] {'tok_0','tok_1',..., dimensions={0} | all-to-all | bytes 3072 | tf_op jit(solution)/shard_map/all_to_all | solution.py:37
  382.7 24.5 %all_to_all.134 = bf16[32,2,3,6,512]{4,1,3,2,0:T(2,128)(2,1)S(1)} all-to-all(bf16[32,2,3,6,512]{4,1,3,2,0:T(2,128)(2,1)S(1)} %broadcast_in_dim.33), channel_id=1, replica_groups=mesh['tok_0'=4,'tok_1'=2,'tok_2'=4,'tok_3'=2,'head'=2] {'tok_0','tok_1',..., dimensions={0} | all-to-all | bytes 2359296 | tf_op jit(solution)/shard_map/all_to_all | solution.py:37
  409.3 5.6 all_to_all.135
  429.6 2.9 maximum_bitcast_fusion.3
  436.1 8.6 %all_to_all.136 = f32[2,32,2,3,6,512]{5,1,4,3,2,0:T(8,128)} all-to-all(f32[2,32,2,3,6,512]{5,1,4,3,2,0:T(8,128)S(1)} %copy.888), channel_id=1, replica_groups=mesh['tok_0'=4,'tok_1'=2,'tok_2'=4,'tok_3'=2,'head'=2] {'tok_3'}, dimensions={0} | all-to-all | bytes 9437184 | tf_op jit(solution)/shard_map/all_to_all | solution.py:23
  444.7 4.6 reduce_sum.223
  449.3 3.5 copy.890
  452.8 37.7 %all_to_all.137 = f32[32,2,3,6,512]{4,1,3,2,0:T(2,128)} all-to-all(f32[32,2,3,6,512]{4,1,3,2,0:T(2,128)S(1)} %copy.890), channel_id=1, replica_groups=mesh['tok_0'=4,'tok_1'=2,'tok_2'=4,'tok_3'=2,'head'=2] {'tok_0','tok_1',..., dimensions={0} | all-to-all | bytes 4718592 | tf_op jit(solution)/shard_map/all_to_all | solution.py:31
  493.1 13.7 %all_to_all.138 = f32[64,2,3]{2,1,0:T(2,128)S(1)} all-to-all(f32[64,2,3]{2,1,0:T(2,128)S(1)} %broadcast_in_dim.35), channel_id=1, replica_groups=mesh['tok_0'=4,'tok_1'=2,'tok_2'=4,'tok_3'=2,'head'=2] {'tok_0','tok_1',..., dimensions={0} | all-to-all | bytes 3072 | tf_op jit(solution)/shard_map/all_to_all | solution.py:37
  509.3 5.3 all-to-all-start.18
  514.6 3.4 fusion.13
  518.0 3.3 convolution_convert_fusion.1
  521.3 4.0 copy.903
  525.3 9.6 %all-to-all-done.18 = bf16[32,2,3,6,512]{4,1,3,2,0:T(2,128)(2,1)S(1)} async-done(((bf16[32,2,3,6,512]{4,1,3,2,0:T(2,128)(2,1)}), bf16[32,2,3,6,512]{4,1,3,2,0:T(2,128)(2,1)S(1)}, u32[]{:S(2)}, u32[]{:S(2)}) %all-to-all-start.18) | async-done | bytes 1179680 | tf_op jit(solution)/shard_map/all_to_all | solution.py:37
  536.9 5.6 all_to_all.139
  552.3 3.1 convolution_convert_fusion
  555.4 3.8 copy.904
  559.2 7.6 %fusion = (f32[2,512]{0,1:T(8,128)S(1)}, bf16[2,512,1024]{2,0,1:T(2,128)(2,1)S(1)}) fusion(bf16[1,512,1024]{2,0,1:T(2,128)(2,1)} %copy.904, bf16[1,512,1024]{2,0,1:T(2,128)(2,1)} %copy.903), kind=kLoop, calls=%fused_computation.8 | loop fusion | flops 7339008 | bytes 4198400 | tf_op jit(solution)/shard_map/reduce_sum | solution.py:125
  567.6 3.2 all-to-all-start.20
  570.8 3.8 all-to-all-done.20
  577.3 27.0 %all_to_all.140 = bf16[2,512,1024]{2,0,1:T(2,128)(2,1)S(1)} all-to-all(bf16[2,512,1024]{2,0,1:T(2,128)(2,1)S(1)} %fusion.2), channel_id=1, replica_groups=mesh['tok_0'=4,'tok_1'=2,'tok_2'=4,'tok_3'=2,'head'=2] {'head'}, dimensions={1} | all-to-all | bytes 4194304 | tf_op jit(solution)/shard_map/all_to_all | solution.py:133
  606.4 2.8 all_to_all.100
  (158 shorter events, 113.7 us)
Async XLA Ops:
  17.0 17.4 %copy-start.2 = (bf16[2,3,384,512]{3,2,1,0:T(8,128)(2,1)S(1)}, bf16[2,3,384,512]{3,2,1,0:T(8,128)(2,1)}, u32[]{:S(2)}) copy-start(bf16[2,3,384,512]{3,2,1,0:T(8,128)(2,1)} %param.8) | copy-start | bytes 7077892
  34.4 4.9 copy-start
  35.3 0.9 copy-start.5
  65.4 45.5 %all-to-all-start.1 = ((f32[32,2,3,6,512]{4,1,3,2,0:T(2,128)}), f32[32,2,3,6,512]{4,1,3,2,0:T(2,128)S(1)}, u32[]{:S(2)}, u32[]{:S(2)}) async-start(f32[32,2,3,6,512]{4,1,3,2,0:T(2,128)} %copy.809), calls=%async_computation.1 | async-start | bytes 4718592 | tf_op jit(solution)/shard_map/all_to_all | solution.py:31
  112.7 13.4 %all-to-all-start.2 = ((f32[64,2,3]{2,1,0:T(2,128)}), f32[64,2,3]{2,1,0:T(2,128)S(1)}, u32[]{:S(2)}, u32[]{:S(2)}) async-start(f32[64,2,3]{2,1,0:T(2,128)} %broadcast_in_dim.26), calls=%async_computation.2 | async-start | bytes 131072 | tf_op jit(solution)/shard_map/all_to_all | solution.py:37
  159.6 5.1 slice-start
  161.3 3.5 slice-start.1
  288.4 2.6 copy-start.1
  288.4 12.6 %slice-start.2 = ((s8[6291456]{0:T(1024)(128)(4,1)}), s8[2097152]{0:T(1024)(128)(4,1)S(1)}, s32[]{:S(2)}) async-start(s8[6291456]{0:T(1024)(128)(4,1)} %bitcast.191), calls=%async_computation.24 | async-start | bytes 4194304
  294.2 6.8 %slice-start.3 = ((s8[6291456]{0:T(1024)(128)(4,1)}), s8[4194304]{0:T(1024)(128)(4,1)S(1)}, s32[]{:S(2)}) async-start(s8[6291456]{0:T(1024)(128)(4,1)} %bitcast.191), calls=%async_computation.25 | async-start | bytes 8388608
  296.5 2.5 copy-start.4
  414.9 5.1 slice-start.4
  416.5 3.5 slice-start.5
  509.3 25.6 %all-to-all-start.18 = ((bf16[32,2,3,6,512]{4,1,3,2,0:T(2,128)(2,1)}), bf16[32,2,3,6,512]{4,1,3,2,0:T(2,128)(2,1)S(1)}, u32[]{:S(2)}, u32[]{:S(2)}) async-start(bf16[32,2,3,6,512]{4,1,3,2,0:T(2,128)(2,1)} %broadcast_in_dim.36), calls=%async_computation.18 | async-start | bytes 2359296 | tf_op jit(solution)/shard_map/all_to_all | solution.py:37
  514.6 3.4 copy-start.3
  559.2 11.6 %copy-start.6 = (f32[2048]{0:T(1024)S(1)}, f32[2048]{0:T(1024)}, u32[]{:S(2)}) copy-start(f32[2048]{0:T(1024)} %param.9) | copy-start | bytes 24580
  567.6 7.0 %all-to-all-start.20 = ((f32[2,2,512]{2,1,0:T(2,128)}), f32[2,2,512]{2,1,0:T(2,128)S(1)}, u32[]{:S(2)}, u32[]{:S(2)}) async-start(f32[2,2,512]{2,1,0:T(2,128)} %broadcast_in_dim.38), calls=%async_computation.20 | async-start | bytes 16384 | tf_op jit(solution)/shard_map/all_to_all | solution.py:37
where the time goes:
time: 615 us; the launch traced here: 609 us
  blocking collectives  311 us (51%)
  local copies, waits for them, and re-layouts  114 us (19%)
  matrix products  56.5 us (9%)
  waiting for transfers between devices  53.4 us (9%)
  other arithmetic  48.8 us (8%)
  starting transfers between devices  24.3 us (4%)
    all_to_all x10, blocking collectives, from_everyone(): lax.all_to_all(jnp.broadcast_to(x[None], (devices, *x.shape)), axis, 0, 0...  137 us
    all_to_all x3, blocking collectives, summed_rows(): lax.all_to_all(nearer, far, split_axis=0, concat_axis=0, tiled=True)  112 us
    dot_general x29, matrix products, mult(): return jnp.einsum(form, left, right, preferred_element_type=jnp.float32)  56.5 us
    all_to_all x4, blocking collectives, sent_and_summed(): pieces = lax.all_to_all(split_up(x, dim, devices), axis, 0, 0, tiled=True)  34.5 us
    all_to_all x1, waiting for transfers between devices, summed_rows(): lax.all_to_all(nearer, far, split_axis=0, concat_axis=0, tiled=True)  32.3 us
    all_to_all x1, blocking collectives, body(): lax.all_to_all(payload, 'head', split_axis=1, concat_axis=2, tiled=True)  27 us
    all_to_all x3, waiting for transfers between devices, from_everyone(): lax.all_to_all(jnp.broadcast_to(x[None], (devices, *x.shape)), axis, 0, 0...  21 us
    reshape x1, local copies, waits for them, and re-layouts, body(): projections.reshape(3, projections.shape[1], local_heads, head_width)  17 us
  transfers between devices with their start and end apart: 4, of which 4 were waited for; matrix products, arithmetic and copies ran while one was open for 2% of the time, Pallas kernels for 0%

commit v1 on v0

v1 whole, which is shorter than its diff:
```python
import functools

import jax
import jax.numpy as jnp
from jax import lax
from jax.experimental import pallas as pl
from jax.experimental.pallas import tpu as pltpu
from jax.sharding import Mesh
from jax.sharding import PartitionSpec as P

INNER = 2
STEP_SIZE = 4.0
EPS = 1e-06
TOK = ("tok_0", "tok_1", "tok_2", "tok_3")
CHIPS = ("tok_0", "tok_1", "tok_2")
PEERS = 32
HD = 512
F = 384
ROWS = 48
COLS = 128
SHARD = 3 * ROWS
NOTE = 16
CHUNK = 256
BF = jnp.bfloat16
F32 = jnp.float32
VMEM_LIMIT = 40 * 1024 * 1024


def params(**more):
    return pltpu.CompilerParams(vmem_limit_bytes=VMEM_LIMIT, **more)


def cost(flops, moved):
    return pl.CostEstimate(flops=int(flops), bytes_accessed=int(moved), transcendentals=0)


def nt(left, right):
    return lax.dot_general(left, right, (((1,), (1,)), ((), ())), preferred_element_type=F32)


def nn(left, right):
    return lax.dot_general(left, right, (((1,), (0,)), ((), ())), preferred_element_type=F32)


def keys_signals_kernel(ids, x_ref, w_ref, rate_ref, out_ref):
    step = pl.program_id(0)
    mapped = nn(x_ref[0], w_ref[0]).astype(BF)

    @pl.when(step < 2)
    def _():
        out_ref[...] = mapped

    @pl.when(step >= 2)
    def _():
        rates = jnp.where(ids[0] == 0, rate_ref[0, :, 0:1], rate_ref[0, :, 1:2])
        out_ref[...] = (-rates * mapped.astype(F32)).astype(BF)


def keys_signals(head, group, inputs, projections, lrate):
    tokens, width = inputs.shape[1:]
    return pl.pallas_call(
        keys_signals_kernel,
        out_shape=jax.ShapeDtypeStruct((tokens, 2 * HD), BF),
        grid_spec=pltpu.PrefetchScalarGridSpec(
            num_scalar_prefetch=1,
            grid=(4,),
            in_specs=[
                pl.BlockSpec((1, tokens, width), lambda j, ids: (group, 0, 0)),
                pl.BlockSpec((1, width, HD // 2), lambda j, ids: (1 + j // 2, 0, 2 * ids[0] + j % 2)),
                pl.BlockSpec((1, tokens, 2), lambda j, ids: (group, 0, 0)),
            ],
            out_specs=pl.BlockSpec((tokens, HD // 2), lambda j, ids: (0, j)),
        ),
        compiler_params=params(),
        cost_estimate=cost(4 * tokens * width * HD, 2 * tokens * width + 4 * width * HD),
    )(head, inputs, projections, lrate)


def queries_kernel(ids, x_ref, w_ref, out_ref):
    out_ref[...] = nn(x_ref[0], w_ref[0]).astype(BF)


def queries_of(head, group, inputs, projections):
    tokens, width = inputs.shape[1:]
    return pl.pallas_call(
        queries_kernel,
        out_shape=jax.ShapeDtypeStruct((tokens, HD), BF),
        grid_spec=pltpu.PrefetchScalarGridSpec(
            num_scalar_prefetch=1,
            grid=(2,),
            in_specs=[
                pl.BlockSpec((1, tokens, width), lambda j, ids: (group, 0, 0)),
                pl.BlockSpec((1, width, HD // 2), lambda j, ids: (0, 0, 2 * ids[0] + j)),
            ],
            out_specs=pl.BlockSpec((tokens, HD // 2), lambda j, ids: (0, j)),
        ),
        compiler_params=params(),
        cost_estimate=cost(2 * tokens * width * HD, 2 * tokens * width + 2 * width * HD),
    )(head, inputs, projections)


def gradients(w_ref, own_ref, other_ref, d_ref, out_ref):
    tokens = own_ref.shape[0]
    for place in range(0, 2 * tokens, CHUNK):
        source = own_ref if place < tokens else other_ref
        first = place % tokens
        keys = source[first : first + CHUNK, 0:HD]
        signals = source[first : first + CHUNK, HD : 2 * HD]
        hidden = nt(w_ref[0:F, :], keys)
        gated = nt(w_ref[F : 2 * F, :], keys)
        back = nt(w_ref[2 * F : 3 * F, :], signals)
        sigma = 0.5 * jnp.tanh(0.5 * hidden) + 0.5
        act = hidden * sigma
        d_ref[0:F, place : place + CHUNK] = (back * gated * (sigma + act * (1.0 - sigma))).astype(BF)
        d_ref[F : 2 * F, place : place + CHUNK] = (back * act).astype(BF)
        d_ref[2 * F : 3 * F, place : place + CHUNK] = (act * gated).astype(BF)
    for m in range(3):
        columns = slice(0, HD) if m < 2 else slice(HD, 2 * HD)
        grad = nn(d_ref[m * F : (m + 1) * F, 0:tokens], own_ref[:, columns])
        grad += nn(d_ref[m * F : (m + 1) * F, tokens : 2 * tokens], other_ref[:, columns])
        grad = grad.astype(BF)
        for r in range(F // ROWS):
            for c in range(HD // COLS):
                out_ref[r * (HD // COLS) + c, m * ROWS : (m + 1) * ROWS, :] = grad[
                    r * ROWS : (r + 1) * ROWS, c * COLS : (c + 1) * COLS
                ]


def renew(w_ref, shards_ref, target_ref, new_ref):
    notes = shards_ref[0, SHARD : SHARD + NOTE, :].astype(F32)
    for i in range(1, PEERS):
        notes += shards_ref[i, SHARD : SHARD + NOTE, :].astype(F32)
    for m in range(3):
        frob = notes[3 * m : 3 * m + 1, :] + notes[3 * m + 1 : 3 * m + 2, :] + notes[3 * m + 2 : 3 * m + 3, :]
        scale = STEP_SIZE * lax.rsqrt(frob + EPS)
        for r in range(F // ROWS):
            rows = slice(m * F + r * ROWS, m * F + (r + 1) * ROWS)
            updates = []
            total = None
            for c in range(HD // COLS):
                grad = shards_ref[r * (HD // COLS) + c, m * ROWS : (m + 1) * ROWS, :].astype(F32)
                update = w_ref[rows, c * COLS : (c + 1) * COLS].astype(F32) - scale * grad
                updates.append(update)
                total = update * update if total is None else total + update * update
            length = jnp.sum(total, axis=1, keepdims=True)
            factor = target_ref[rows, :] * lax.rsqrt(length + EPS)
            for c in range(HD // COLS):
                new_ref[rows, c * COLS : (c + 1) * COLS] = (updates[c] * factor).astype(BF)


def first_step_kernel(ids, init_ref, own_ref, other_ref, out_ref, w_ref, target_ref, d_ref):
    for m in range(3):
        rows = slice(m * F, (m + 1) * F)
        start = init_ref[0, m]
        w_ref[rows, :] = start
        start = start.astype(F32)
        length = jnp.sqrt(jnp.sum(start * start, axis=1, keepdims=True))
        target_ref[rows, :] = jnp.broadcast_to(length, (F, COLS))
    gradients(w_ref, own_ref, other_ref, d_ref, out_ref)


def next_step_kernel(old_ref, shards_ref, target_ref, own_ref, other_ref, out_ref, w_ref, d_ref):
    renew(old_ref, shards_ref, target_ref, w_ref)
    gradients(w_ref, own_ref, other_ref, d_ref, out_ref)


GRADS = jax.ShapeDtypeStruct((PEERS, SHARD, COLS), BF)
MEMORY = jax.ShapeDtypeStruct((3 * F, HD), BF)
TARGET = jax.ShapeDtypeStruct((3 * F, COLS), F32)


def first_step(core, fast_init, own, other):
    tokens = own.shape[0]
    whole = pl.BlockSpec((tokens, 2 * HD), lambda i, ids: (0, 0))
    return pl.pallas_call(
        first_step_kernel,
        out_shape=(GRADS, MEMORY, TARGET),
        grid_spec=pltpu.PrefetchScalarGridSpec(
            num_scalar_prefetch=1,
            grid=(1,),
            in_specs=[pl.BlockSpec((1, 3, F, HD), lambda i, ids: (ids[0], 0, 0, 0)), whole, whole],
            out_specs=(
                pl.BlockSpec(GRADS.shape, lambda i, ids: (0, 0, 0)),
                pl.BlockSpec(MEMORY.shape, lambda i, ids: (0, 0)),
                pl.BlockSpec(TARGET.shape, lambda i, ids: (0, 0)),
            ),
            scratch_shapes=[pltpu.VMEM((3 * F, 2 * tokens), BF)],
        ),
        compiler_params=params(),
        cost_estimate=cost(24 * tokens * F * HD, 8 << 20),
    )(core, fast_init, own, other)


def next_step(old, shards, target, own, other):
    tokens = own.shape[0]
    return pl.pallas_call(
        next_step_kernel,
        out_shape=(GRADS, MEMORY),
        scratch_shapes=[pltpu.VMEM((3 * F, 2 * tokens), BF)],
        compiler_params=params(),
        cost_estimate=cost(24 * tokens * F * HD, 8 << 20),
    )(old, shards, target, own, other)


def sum_kernel(parts_ref, out_ref):
    total = parts_ref[0].astype(F32)
    for i in range(1, PEERS):
        total += parts_ref[i].astype(F32)
    row = lax.broadcasted_iota(jnp.int32, (NOTE, COLS), 0)
    notes = jnp.zeros((NOTE, COLS), F32)
    for m in range(3):
        part = total[m * ROWS : (m + 1) * ROWS, :]
        left = jnp.broadcast_to(jnp.sum(part * part, keepdims=True), (NOTE, COLS))
        for piece in range(3):
            term = left.astype(BF).astype(F32)
            notes = jnp.where(row == 3 * m + piece, term, notes)
            left = left - term
    total = total.astype(BF)
    notes = notes.astype(BF)
    for i in range(PEERS):
        out_ref[i, 0:SHARD, :] = total
        out_ref[i, SHARD : SHARD + NOTE, :] = notes


def sum_shards(parts):
    return pl.pallas_call(
        sum_kernel,
        out_shape=jax.ShapeDtypeStruct((PEERS, SHARD + NOTE, COLS), BF),
        compiler_params=params(),
        cost_estimate=cost(2 * parts.size, 4 * parts.size),
    )(parts)


def exchange(x):
    return lax.all_to_all(x, CHIPS, 0, 0, tiled=True)


def read(w_ref, queries):
    hidden = nt(queries, w_ref[0:F, :])
    gated = nt(queries, w_ref[F : 2 * F, :])
    sigma = 0.5 * jnp.tanh(0.5 * hidden) + 0.5
    mixed = (hidden * sigma * gated).astype(BF)
    return nn(mixed, w_ref[2 * F : 3 * F, :]).astype(BF)


def read_kernel(ids, w_ref, own_ref, other_ref, own_out, other_out):
    own_out[...] = read(w_ref, own_ref[...])
    other_out[...] = read(w_ref, other_ref[...])


def renew_read_kernel(ids, old_ref, shards_ref, target_ref, own_ref, other_ref, own_out, other_out, w_ref):
    renew(old_ref, shards_ref, target_ref, w_ref)
    own_out[...] = read(w_ref, own_ref[...])
    other_out[...] = read(w_ref, other_ref[...])


def read_half(half, memory, own, other):
    tokens = own.shape[0] // 2
    part = pl.BlockSpec((tokens, HD), lambda i, ids: (ids[0], 0))
    back = pl.BlockSpec((tokens, HD), lambda i, ids: (0, 0))
    out = jax.ShapeDtypeStruct((tokens, HD), BF)
    fixed = [pl.BlockSpec(x.shape, lambda i, ids, n=x.ndim: (0,) * n) for x in memory]
    renewed = len(memory) > 1
    return pl.pallas_call(
        renew_read_kernel if renewed else read_kernel,
        out_shape=(out, out, MEMORY) if renewed else (out, out),
        grid_spec=pltpu.PrefetchScalarGridSpec(
            num_scalar_prefetch=1,
            grid=(1,),
            in_specs=[*fixed, part, part],
            out_specs=(back, back, pl.BlockSpec(MEMORY.shape, lambda i, ids: (0, 0))) if renewed else (back, back),
        ),
        compiler_params=params(),
        cost_estimate=cost(12 * tokens * F * HD, 4 << 20),
    )(half, *memory, own, other)


def norm_kernel(ids, a_ref, b_ref, c_ref, d_ref, gain_ref, *rest):
    out_ref = rest[-1]
    core, far = ids[0], ids[1]
    pieces = (a_ref, b_ref, c_ref, d_ref)
    heads = (2 * far + core, 2 * far + 1 - core, 2 * (1 - far) + core, 2 * (1 - far) + 1 - core)
    total = None
    for piece in pieces:
        value = piece[...].astype(F32)
        square = jnp.sum(value * value, axis=1, keepdims=True)
        total = square if total is None else total + square
    scale = lax.rsqrt(total / (4 * HD) + EPS)
    for piece, head in zip(pieces, heads):
        columns = pl.ds(pl.multiple_of(head * HD, HD), HD)
        out_ref[0, :, columns] = (piece[...].astype(F32) * scale * gain_ref[0:1, columns]).astype(BF)


def normalise(ids, group, groups, pieces, gain, former):
    tokens = pieces[0].shape[0]
    part = pl.BlockSpec((tokens, HD), lambda i, ids: (0, 0))
    more = [] if former is None else [former]
    return pl.pallas_call(
        norm_kernel,
        out_shape=jax.ShapeDtypeStruct((groups, tokens, 4 * HD), BF),
        grid_spec=pltpu.PrefetchScalarGridSpec(
            num_scalar_prefetch=1,
            grid=(1,),
            in_specs=[part] * 4
            + [pl.BlockSpec((1, 4 * HD), lambda i, ids: (0, 0))]
            + [pl.BlockSpec(memory_space=pl.ANY)] * len(more),
            out_specs=pl.BlockSpec((1, tokens, 4 * HD), lambda i, ids: (group, 0, 0)),
        ),
        input_output_aliases={} if former is None else {6: 0},
        compiler_params=params(),
        cost_estimate=cost(8 * tokens * HD * 4, 4 * tokens * HD * 4),
    )(ids, *pieces, gain, *more)


def body(inputs, projections, lrate, fast_init, gain):
    groups = inputs.shape[0]
    core = lax.axis_index("tok_3").astype(jnp.int32)
    far = lax.axis_index("head").astype(jnp.int32)
    mine = core.reshape(1)
    mates = (1 - core).reshape(1)
    near_half = far.reshape(1)
    far_half = (1 - far).reshape(1)
    ids = jnp.stack([core, far])
    gain = gain.reshape(1, -1)
    swap = [(0, 1), (1, 0)]
    both = [(0, 3), (1, 2), (2, 1), (3, 0)]

    def swapped(x):
        return lax.ppermute(x, "tok_3", swap)

    def pairs(group, dep=None):
        x, w = inputs, projections
        start, later = mates, mine
        if dep is not None:
            start, later, _ = lax.optimization_barrier((mates, mine, dep))
        other = swapped(keys_signals(start, group, x, w, lrate))
        own = keys_signals(later, group, x, w, lrate)
        return own, other

    def asks(group, dep):
        start, later, _ = lax.optimization_barrier((mates, mine, dep))
        other = swapped(queries_of(start, group, inputs, projections))
        own = queries_of(later, group, inputs, projections)
        return own, other

    def finish(group, far_parts, near_parts, former):
        ahead = lax.ppermute(far_parts[0], "head", swap)
        across = lax.ppermute(far_parts[1], ("tok_3", "head"), both)
        beside = swapped(near_parts[1])
        return normalise(ids, group, groups, (near_parts[0], beside, ahead, across), gain, former)

    result = None
    pair = pairs(0)
    grads, memory, target = first_step(mine, fast_init, *pair)
    asked = None
    for group in range(groups):
        for inner in range(INNER):
            if inner == 0:
                asked = asks(group, grads)
            elif group + 1 < groups:
                later_pair = pairs(group + 1, grads)
            shards = exchange(sum_shards(exchange(grads)))
            if inner + 1 < INNER:
                grads, memory = next_step(memory, shards, target, *pair)
            elif group + 1 < groups:
                pair = later_pair
                grads, memory = next_step(memory, shards, target, *pair)
                far_parts = read_half(far_half, (memory,), *asked)
                near_parts = read_half(near_half, (memory,), *asked)
                result = finish(group, far_parts, near_parts, result)
            else:
                *far_parts, memory = read_half(far_half, (memory, shards, target), *asked)
                near_parts = read_half(near_half, (memory,), *asked)
                result = finish(group, far_parts, near_parts, result)
    return result


def solution(mesh):
    finer = Mesh(
        mesh.devices.reshape(4, 2, 4, 2, mesh.shape["head"]),
        ("tok_0", "tok_1", "tok_2", "tok_3", "head"),
    )
    placed = (
        P(None, TOK, None),
        P(None, None, "head"),
        P(None, TOK, "head"),
        P("head", None, None, None),
        P(),
    )
    return jax.shard_map(
        body, mesh=finer, in_specs=placed, out_specs=P(None, (*TOK, "head"), None), check_vma=False
    )
```

time: 615 us -> 261 us (0.42)
  blocking collectives: 311 us -> 152 us
  local copies, waits for them, and re-layouts: 114 us -> 15.3 us
  Pallas kernels: 0 us -> 63 us
  matrix products: 56.5 us -> 0 us
  other arithmetic: 48.8 us -> 0.07 us
  waiting for transfers between devices: 53.4 us -> 12.8 us
  starting transfers between devices: 24.3 us -> 15.1 us
    all_to_all x18 -> x6, blocking collectives: 311 us -> 152 us  [exchange(): return lax.all_to_all(x, CHIPS, 0, 0, tiled=True)]
    pallas_call x0 -> x22, Pallas kernels: none -> 63 us  [the longest x4 21.3 us: keys_signals(): pl.pallas_call(keys_signals_kernel, out_shape=jax.ShapeDtypeStruct((token...]
    dot_general x29 -> x0, matrix products: 56.5 us -> none  [mult(): return jnp.einsum(form, left, right, preferred_element_type=jnp.float32)]
    all_to_all x4 -> x2, waiting for transfers between devices: 53.4 us -> 4.07 us  [exchange(): return lax.all_to_all(x, CHIPS, 0, 0, tiled=True)]
    reduce_sum x23 -> x0, other arithmetic: 34 us -> none  [the longest x4 15.5 us: sent_and_summed(): return jnp.sum(pieces, axis=0)]
    transpose x16 -> x0, local copies, waits for them, and re-layouts: 28.4 us -> none  [the longest x8 15.4 us: split_up(): return jnp.moveaxis(pieces, dim, 0)]
    reshape x1 -> x0, local copies, waits for them, and re-layouts: 17 us -> none  [body(): projections.reshape(3, projections.shape[1], local_heads, head_width)]
    dot_general x12 -> x0, local copies, waits for them, and re-layouts: 14.6 us -> none  [mult(): return jnp.einsum(form, left, right, preferred_element_type=jnp.float32)]
  transfers between devices with their start and end apart: 4 -> 12, of which waited for: 4 -> 3; matrix products, arithmetic and copies ran while one was open for 2% -> 0% of each run, Pallas kernels for 0% -> 15%
where the time goes in v1:
time: 261 us; the launch traced here: 259 us
  blocking collectives  152 us (58%)
  Pallas kernels  63 us (24%)
  local copies, waits for them, and re-layouts  15.3 us (6%)
  starting transfers between devices  15.1 us (6%)
  waiting for transfers between devices  12.8 us (5%)
    all_to_all x6, blocking collectives, exchange(): return lax.all_to_all(x, CHIPS, 0, 0, tiled=True)  152 us
    pallas_call x4, Pallas kernels, keys_signals(): pl.pallas_call(keys_signals_kernel, out_shape=jax.ShapeDtypeStruct((token...  21.3 us
    unnamed x47, local copies, waits for them, and re-layouts  15.3 us
    pallas_call x4, Pallas kernels, queries_of(): pl.pallas_call(queries_kernel, out_shape=jax.ShapeDtypeStruct((tokens, HD...  11.6 us
    all_to_all x2, starting transfers between devices, exchange(): return lax.all_to_all(x, CHIPS, 0, 0, tiled=True)  10.1 us
    pallas_call x3, Pallas kernels, next_step(): pl.pallas_call(next_step_kernel, out_shape=(GRADS, MEMORY), scratch_shape...  10 us
    pallas_call x4, Pallas kernels, read_half(): pl.pallas_call(renew_read_kernel if renewed else read_kernel, out_shape=(...  8.63 us
  transfers between devices with their start and end apart: 12, of which 3 were waited for; matrix products, arithmetic and copies ran while one was open for 0% of the time, Pallas kernels for 15%

profile of v1, /device:TPU:2, one launch (start us, length us, event | category | flops | bytes accessed | tf_op | source)
XLA Modules:
  0.0 258.9 jit_solution(10697260191849304361)
XLA Ops:
  0.0 0.9 copy.7.rate_ref
  0.9 2.2 copy-done
  3.1 5.3 %shard_map.56 = bf16[512,1024]{1,0:T(8,128)(2,1)S(1)} custom-call(s32[1]{0:T(128)} %bitcast.3.ids, bf16[2,512,2048]{2,1,0:T(8,128)(2,1)S(1)} %copy-done, bf16[3,2048,1024]{2,1,0:T(8,128)(2,1)} %w_ref.15, f32[2,512,2]{2,1,0:T(8,128)S(1)} %copy.7.rate_ref), custom_call_target="tpu_custom_call" | custom-call | flops 2147483648 | bytes 6291456 | tf_op jit(solution)/shard_map/pallas_call | solution.py:61
  8.6 5.4 %shard_map.55.own_ref = bf16[512,1024]{1,0:T(8,128)(2,1)S(1)} custom-call(s32[1]{0:T(128)} %bitcast.ids, bf16[2,512,2048]{2,1,0:T(8,128)(2,1)S(1)} %copy-done.1, bf16[3,2048,1024]{2,1,0:T(8,128)(2,1)} %w_ref.15, f32[2,512,2]{2,1,0:T(8,128)S(1)} %copy.7.rate_ref), custom_call_target="tpu_custom_call" | custom-call | flops 2147483648 | bytes 6291456 | tf_op jit(solution)/shard_map/pallas_call | solution.py:61
  14.0 2.9 %shard_map.57 = (bf16[32,144,128]{2,1,0:T(8,128)(2,1)S(1)}, bf16[1152,512]{1,0:T(8,128)(2,1)S(1)}, f32[1152,128]{1,0:T(8,128)S(1)}) custom-call(s32[1]{0:T(128)} %bitcast.ids, bf16[2,3,384,512]{3,2,1,0:T(8,128)(2,1)S(1)} %copy-done.15, bf16[512,1024]{1,0:T(8,128)(2,1)S(1)} %shard_map.55.own_ref, bf16[512,1024]{1,0:T(8,128)(2,1)S(1)} %collective-permute-done.other_ref), custom_call_target="tpu_custom_call" | custom-call | flops 2415919104 | bytes 8388608 | tf_op jit(solution)/shard_map/pallas_call | solution.py:175
  16.9 30.9 %all_to_all.40.parts_ref = bf16[32,144,128]{2,1,0:T(8,128)(2,1)S(1)} all-to-all(bf16[32,144,128]{2,1,0:T(8,128)(2,1)S(1)} %get-tuple-element.30), channel_id=1, replica_groups=mesh['tok_0'=4,'tok_1'=2,'tok_2'=4,'tok_3'=2,'head'=2] {'tok_0','tok_1',..., dimensions={0} | all-to-all | bytes 2359296 | tf_op jit(solution)/shard_map/all_to_all | solution.py:235
  47.8 0.3 shard_map.58
  48.1 24.9 %all_to_all.41.shards_ref = bf16[32,160,128]{2,1,0:T(8,128)(2,1)S(1)} all-to-all(bf16[32,160,128]{2,1,0:T(8,128)(2,1)S(1)} %shard_map.58), channel_id=1, replica_groups=mesh['tok_0'=4,'tok_1'=2,'tok_2'=4,'tok_3'=2,'head'=2] {'tok_0','tok_1',..., dimensions={0} | all-to-all | bytes 2621440 | tf_op jit(solution)/shard_map/all_to_all | solution.py:235
  73.0 3.4 %shard_map.59 = (bf16[32,144,128]{2,1,0:T(8,128)(2,1)S(1)}, bf16[1152,512]{1,0:T(8,128)(2,1)S(1)}) custom-call(bf16[1152,512]{1,0:T(8,128)(2,1)S(1)} %get-tuple-element.29.old_ref, bf16[32,160,128]{2,1,0:T(8,128)(2,1)S(1)} %all_to_all.41.shards_ref, f32[1152,128]{1,0:T(8,128)S(1)} %get-tuple-element.31.target_ref, bf16[512,1024]{1,0:T(8,128)(2,1)S(1)} %shard_map.55.own_ref, ...), custom_call_target="tpu_custom_call" | custom-call | flops 2415919104 | bytes 8388608 | tf_op jit(solution)/shard_map/pallas_call | solution.py:196
  76.4 1.0 copy-done.21
  77.5 22.8 %all_to_all.42.parts_ref = bf16[32,144,128]{2,1,0:T(8,128)(2,1)S(1)} all-to-all(bf16[32,144,128]{2,1,0:T(8,128)(2,1)S(1)} %get-tuple-element.33), channel_id=1, replica_groups=mesh['tok_0'=4,'tok_1'=2,'tok_2'=4,'tok_3'=2,'head'=2] {'tok_0','tok_1',..., dimensions={0} | all-to-all | bytes 2359296 | tf_op jit(solution)/shard_map/all_to_all | solution.py:235
  100.2 1.4 shard_map.60
  101.6 5.1 %all-to-all-start.3 = ((bf16[32,160,128]{2,1,0:T(8,128)(2,1)}), bf16[32,160,128]{2,1,0:T(8,128)(2,1)S(1)}, u32[]{:S(2)}, u32[]{:S(2)}) async-start(bf16[32,160,128]{2,1,0:T(8,128)(2,1)} %shard_map.60), calls=%async_computation.3 | async-start | bytes 2621440 | tf_op jit(solution)/shard_map/all_to_all | solution.py:235
  106.7 2.2 copy-done.2
  108.9 5.3 %shard_map.62 = bf16[512,1024]{1,0:T(8,128)(2,1)S(1)} custom-call(s32[1]{0:T(128)} %bitcast.3.ids, bf16[2,512,2048]{2,1,0:T(8,128)(2,1)S(1)} %copy-done.2, bf16[3,2048,1024]{2,1,0:T(8,128)(2,1)} %w_ref.15, f32[2,512,2]{2,1,0:T(8,128)S(1)} %copy.7.rate_ref), custom_call_target="tpu_custom_call" | custom-call | flops 2147483648 | bytes 6291456 | tf_op jit(solution)/shard_map/pallas_call | solution.py:61
  114.5 5.2 %shard_map.61.own_ref = bf16[512,1024]{1,0:T(8,128)(2,1)S(1)} custom-call(s32[1]{0:T(128)} %bitcast.ids, bf16[2,512,2048]{2,1,0:T(8,128)(2,1)S(1)} %copy-done.3, bf16[3,2048,1024]{2,1,0:T(8,128)(2,1)} %w_ref.15, f32[2,512,2]{2,1,0:T(8,128)S(1)} %copy.7.rate_ref), custom_call_target="tpu_custom_call" | custom-call | flops 2147483648 | bytes 6291456 | tf_op jit(solution)/shard_map/pallas_call | solution.py:61
  119.7 1.0 copy-done.16
  120.7 4.1 %all-to-all-done.3.shards_ref = bf16[32,160,128]{2,1,0:T(8,128)(2,1)S(1)} async-done(((bf16[32,160,128]{2,1,0:T(8,128)(2,1)}), bf16[32,160,128]{2,1,0:T(8,128)(2,1)S(1)}, u32[]{:S(2)}, u32[]{:S(2)}) %all-to-all-start.3) | async-done | bytes 1310752 | tf_op jit(solution)/shard_map/all_to_all | solution.py:235
  124.8 1.2 copy-done.17
  126.0 1.3 copy-done.22
  127.3 3.3 %shard_map.63 = (bf16[32,144,128]{2,1,0:T(8,128)(2,1)S(1)}, bf16[1152,512]{1,0:T(8,128)(2,1)S(1)}) custom-call(bf16[1152,512]{1,0:T(8,128)(2,1)S(1)} %copy-done.22, bf16[32,160,128]{2,1,0:T(8,128)(2,1)S(1)} %all-to-all-done.3.shards_ref, f32[1152,128]{1,0:T(8,128)S(1)} %get-tuple-element.31.target_ref, bf16[512,1024]{1,0:T(8,128)(2,1)S(1)} %shard_map.61.own_ref, ...), custom_call_target="tpu_custom_call" | custom-call | flops 2415919104 | bytes 8388608 | tf_op jit(solution)/shard_map/pallas_call | solution.py:196
  130.6 25.8 %all_to_all.43.parts_ref = bf16[32,144,128]{2,1,0:T(8,128)(2,1)S(1)} all-to-all(bf16[32,144,128]{2,1,0:T(8,128)(2,1)S(1)} %get-tuple-element.37), channel_id=1, replica_groups=mesh['tok_0'=4,'tok_1'=2,'tok_2'=4,'tok_3'=2,'head'=2] {'tok_0','tok_1',..., dimensions={0} | all-to-all | bytes 2359296 | tf_op jit(solution)/shard_map/all_to_all | solution.py:235
  156.8 25.0 %all_to_all.44.shards_ref = bf16[32,160,128]{2,1,0:T(8,128)(2,1)S(1)} all-to-all(bf16[32,160,128]{2,1,0:T(8,128)(2,1)S(1)} %shard_map.64), channel_id=1, replica_groups=mesh['tok_0'=4,'tok_1'=2,'tok_2'=4,'tok_3'=2,'head'=2] {'tok_0','tok_1',..., dimensions={0} | all-to-all | bytes 2621440 | tf_op jit(solution)/shard_map/all_to_all | solution.py:235
  181.8 3.3 %shard_map.65 = (bf16[32,144,128]{2,1,0:T(8,128)(2,1)S(1)}, bf16[1152,512]{1,0:T(8,128)(2,1)S(1)}) custom-call(bf16[1152,512]{1,0:T(8,128)(2,1)S(1)} %get-tuple-element.36.old_ref.w_ref, bf16[32,160,128]{2,1,0:T(8,128)(2,1)S(1)} %all_to_all.44.shards_ref, f32[1152,128]{1,0:T(8,128)S(1)} %copy-done.10, bf16[512,1024]{1,0:T(8,128)(2,1)S(1)} %copy-done.8, ...), custom_call_target="tpu_custom_call" | custom-call | flops 2415919104 | bytes 8388608 | tf_op jit(solution)/shard_map/pallas_call | solution.py:196
  185.2 22.8 %all_to_all.45.parts_ref = bf16[32,144,128]{2,1,0:T(8,128)(2,1)S(1)} all-to-all(bf16[32,144,128]{2,1,0:T(8,128)(2,1)S(1)} %get-tuple-element.39), channel_id=1, replica_groups=mesh['tok_0'=4,'tok_1'=2,'tok_2'=4,'tok_3'=2,'head'=2] {'tok_0','tok_1',..., dimensions={0} | all-to-all | bytes 2359296 | tf_op jit(solution)/shard_map/all_to_all | solution.py:235
  207.9 1.4 shard_map.66
  209.3 5.1 %all-to-all-start.7 = ((bf16[32,160,128]{2,1,0:T(8,128)(2,1)}), bf16[32,160,128]{2,1,0:T(8,128)(2,1)S(1)}, u32[]{:S(2)}, u32[]{:S(2)}) async-start(bf16[32,160,128]{2,1,0:T(8,128)(2,1)} %shard_map.66), calls=%async_computation.7 | async-start | bytes 2621440 | tf_op jit(solution)/shard_map/all_to_all | solution.py:235
  214.4 2.2 copy-done.4
  216.6 2.7 %shard_map.72 = bf16[512,512]{1,0:T(8,128)(2,1)S(1)} custom-call(s32[1]{0:T(128)} %bitcast.3.ids, bf16[2,512,2048]{2,1,0:T(8,128)(2,1)S(1)} %copy-done.4, bf16[3,2048,1024]{2,1,0:T(8,128)(2,1)} %w_ref.15), custom_call_target="tpu_custom_call" | custom-call | flops 1073741824 | bytes 4194304 | tf_op jit(solution)/shard_map/pallas_call | solution.py:85
  219.4 3.4 %shard_map.68 = bf16[512,512]{1,0:T(8,128)(2,1)} custom-call(s32[1]{0:T(128)} %bitcast.3.ids, bf16[2,512,2048]{2,1,0:T(8,128)(2,1)S(1)} %copy-done.4, bf16[3,2048,1024]{2,1,0:T(8,128)(2,1)} %w_ref.15), custom_call_target="tpu_custom_call" | custom-call | flops 1073741824 | bytes 4194304 | tf_op jit(solution)/shard_map/pallas_call | solution.py:85
  222.8 0.5 collective-permute-start.2
  223.2 2.2 copy-done.5
  225.4 2.8 %shard_map.71.own_ref = bf16[512,512]{1,0:T(8,128)(2,1)S(1)} custom-call(s32[1]{0:T(128)} %bitcast.ids, bf16[2,512,2048]{2,1,0:T(8,128)(2,1)S(1)} %copy-done.5, bf16[3,2048,1024]{2,1,0:T(8,128)(2,1)} %w_ref.15), custom_call_target="tpu_custom_call" | custom-call | flops 1073741824 | bytes 4194304 | tf_op jit(solution)/shard_map/pallas_call | solution.py:85
  228.3 3.0 %shard_map.74 = (bf16[256,512]{1,0:T(8,128)(2,1)}, bf16[256,512]{1,0:T(8,128)(2,1)}) custom-call(s32[1]{0:T(128)} %bitcast.2.ids, bf16[1152,512]{1,0:T(8,128)(2,1)S(1)} %copy-done.20, bf16[512,512]{1,0:T(8,128)(2,1)S(1)} %shard_map.71.own_ref, bf16[512,512]{1,0:T(8,128)(2,1)} %collective-permute-done.6.other_ref), custom_call_target="tpu_custom_call" | custom-call | flops 603979776 | bytes 4194304 | tf_op jit(solution)/shard_map/pallas_call | solution.py:264
  231.2 1.0 collective-permute-start.8
  232.2 0.4 collective-permute-start.9
  232.6 2.8 %shard_map.73 = (bf16[256,512]{1,0:T(8,128)(2,1)S(1)}, bf16[256,512]{1,0:T(8,128)(2,1)}) custom-call(s32[1]{0:T(128)} %bitcast.1.ids, bf16[1152,512]{1,0:T(8,128)(2,1)S(1)} %copy-done.20, bf16[512,512]{1,0:T(8,128)(2,1)S(1)} %shard_map.71.own_ref, bf16[512,512]{1,0:T(8,128)(2,1)} %collective-permute-done.6.other_ref), custom_call_target="tpu_custom_call" | custom-call | flops 603979776 | bytes 4194304 | tf_op jit(solution)/shard_map/pallas_call | solution.py:264
  235.4 0.8 collective-permute-start.7
  236.2 2.7 %shard_map.67.own_ref = bf16[512,512]{1,0:T(8,128)(2,1)S(1)} custom-call(s32[1]{0:T(128)} %bitcast.ids, bf16[2,512,2048]{2,1,0:T(8,128)(2,1)S(1)} %copy-done.6, bf16[3,2048,1024]{2,1,0:T(8,128)(2,1)} %w_ref.15), custom_call_target="tpu_custom_call" | custom-call | flops 1073741824 | bytes 4194304 | tf_op jit(solution)/shard_map/pallas_call | solution.py:85
  238.9 1.1 copy-done.11
  240.0 1.7 shard_map.69
  241.7 1.2 shard_map.70
  243.1 1.0 collective-permute-start.4
  244.1 0.8 collective-permute-start.5
  245.0 3.2 %shard_map.75.rest_0_ = bf16[2,256,2048]{2,1,0:T(8,128)(2,1)} custom-call(s32[2]{0:T(128)S(1)} %pad_add_fusion.ids, bf16[256,512]{1,0:T(8,128)(2,1)S(1)} %copy-done.13, bf16[256,512]{1,0:T(8,128)(2,1)} %collective-permute-done.7.b_ref, bf16[256,512]{1,0:T(8,128)(2,1)} %collective-permute-done.8.c_ref, bf16[256,512]{1,0:T(8,128)(2,1)} %collective-permute-done.9.d_ref, ...), custom_call_target="tpu_custom_call" | custom-call | flops 4194304 | bytes 2097152 | tf_op jit(solution)/shard_map/pallas_call | solution.py:298
  248.1 4.1 %collective-permute-done.4.c_ref = bf16[256,512]{1,0:T(8,128)(2,1)S(1)} collective-permute-done((bf16[256,512]{1,0:T(8,128)(2,1)S(1)}, bf16[256,512]{1,0:T(8,128)(2,1)S(1)}, u32[]{:S(2)}, u32[]{:S(2)}) %collective-permute-start.4) | collective-permute-done | bytes 262176 | tf_op jit(solution)/shard_map/ppermute | solution.py:347
  252.2 4.7 %collective-permute-done.5.d_ref = bf16[256,512]{1,0:T(8,128)(2,1)S(1)} collective-permute-done((bf16[256,512]{1,0:T(8,128)(2,1)S(1)}, bf16[256,512]{1,0:T(8,128)(2,1)S(1)}, u32[]{:S(2)}, u32[]{:S(2)}) %collective-permute-start.5) | collective-permute-done | bytes 262176 | tf_op jit(solution)/shard_map/ppermute | solution.py:348
  256.9 2.1 shard_map.76
  (52 shorter events, 1.1 us)
Async XLA Ops:
  0.9 2.2 copy-start
  3.1 5.4 %copy-start.1 = (bf16[2,512,2048]{2,1,0:T(8,128)(2,1)S(1)}, bf16[2,512,2048]{2,1,0:T(8,128)(2,1)}, u32[]{:S(2)}) copy-start(bf16[2,512,2048]{2,1,0:T(8,128)(2,1)} %x_ref.15) | copy-start | bytes 12582916
  8.5 5.5 %collective-permute-start = (bf16[512,1024]{1,0:T(8,128)(2,1)S(1)}, bf16[512,1024]{1,0:T(8,128)(2,1)S(1)}, u32[]{:S(2)}, u32[]{:S(2)}) collective-permute-start(bf16[512,1024]{1,0:T(8,128)(2,1)S(1)} %shard_map.56), channel_id=1, source_target_pairs={{0,2},{2,0},{1,3},{3,1},{4,6},{6,4},{5,7},{7,5},{8,10},{10,8},{9,1... | collective-permute-start | bytes 3145736 | tf_op jit(solution)/shard_map/ppermute | solution.py:329
  8.6 5.4 %copy-start.15 = (bf16[2,3,384,512]{3,2,1,0:T(8,128)(2,1)S(1)}, bf16[2,3,384,512]{3,2,1,0:T(8,128)(2,1)}, u32[]{:S(2)}) copy-start(bf16[2,3,384,512]{3,2,1,0:T(8,128)(2,1)} %init_ref.1) | copy-start | bytes 7077892
  16.9 107.9 %copy-start.9 = (f32[1152,128]{1,0:T(8,128)}, f32[1152,128]{1,0:T(8,128)S(1)}, u32[]{:S(2)}) copy-start(f32[1152,128]{1,0:T(8,128)S(1)} %get-tuple-element.31.target_ref) | copy-start | bytes 1769476
  76.4 1.0 copy-start.21
  101.6 23.2 %all-to-all-start.3 = ((bf16[32,160,128]{2,1,0:T(8,128)(2,1)}), bf16[32,160,128]{2,1,0:T(8,128)(2,1)S(1)}, u32[]{:S(2)}, u32[]{:S(2)}) async-start(bf16[32,160,128]{2,1,0:T(8,128)(2,1)} %shard_map.60), calls=%async_computation.3 | async-start | bytes 2621440 | tf_op jit(solution)/shard_map/all_to_all | solution.py:235
  106.7 2.2 copy-start.2
  108.9 5.6 %copy-start.3 = (bf16[2,512,2048]{2,1,0:T(8,128)(2,1)S(1)}, bf16[2,512,2048]{2,1,0:T(8,128)(2,1)}, u32[]{:S(2)}) copy-start(bf16[2,512,2048]{2,1,0:T(8,128)(2,1)} %x_ref.15) | copy-start | bytes 12582916
  114.2 5.5 %collective-permute-start.1 = (bf16[512,1024]{1,0:T(8,128)(2,1)S(1)}, bf16[512,1024]{1,0:T(8,128)(2,1)S(1)}, u32[]{:S(2)}, u32[]{:S(2)}) collective-permute-start(bf16[512,1024]{1,0:T(8,128)(2,1)S(1)} %shard_map.62), channel_id=1, source_target_pairs={{0,2},{2,0},{1,3},{3,1},{4,6},{6,4},{5,7},{7,5},{8,10},{10,8},{9,1... | collective-permute-start | bytes 3145736 | tf_op jit(solution)/shard_map/ppermute | solution.py:329
  119.7 10.9 %copy-start.7 = (bf16[512,1024]{1,0:T(8,128)(2,1)}, bf16[512,1024]{1,0:T(8,128)(2,1)S(1)}, u32[]{:S(2)}) copy-start(bf16[512,1024]{1,0:T(8,128)(2,1)S(1)} %shard_map.61.own_ref) | copy-start | bytes 3145732
  119.7 1.0 copy-start.16
  124.8 1.2 copy-start.17
  126.0 1.3 copy-start.22
  130.6 51.2 %copy-start.19 = (bf16[1152,512]{1,0:T(8,128)(2,1)}, bf16[1152,512]{1,0:T(8,128)(2,1)S(1)}, u32[]{:S(2)}) copy-start(bf16[1152,512]{1,0:T(8,128)(2,1)S(1)} %get-tuple-element.36.old_ref.w_ref) | copy-start | bytes 3538948
  156.5 25.4 %copy-start.18 = (bf16[512,1024]{1,0:T(8,128)(2,1)S(1)}, bf16[512,1024]{1,0:T(8,128)(2,1)}, u32[]{:S(2)}) copy-start(bf16[512,1024]{1,0:T(8,128)(2,1)} %copy-done.16) | copy-start | bytes 3145732
  156.8 25.1 %copy-start.8 = (bf16[512,1024]{1,0:T(8,128)(2,1)S(1)}, bf16[512,1024]{1,0:T(8,128)(2,1)}, u32[]{:S(2)}) copy-start(bf16[512,1024]{1,0:T(8,128)(2,1)} %copy-done.7) | copy-start | bytes 3145732
  156.8 25.1 %copy-start.10 = (f32[1152,128]{1,0:T(8,128)S(1)}, f32[1152,128]{1,0:T(8,128)}, u32[]{:S(2)}) copy-start(f32[1152,128]{1,0:T(8,128)} %copy-done.9) | copy-start | bytes 1769476
  209.3 29.6 %all-to-all-start.7 = ((bf16[32,160,128]{2,1,0:T(8,128)(2,1)}), bf16[32,160,128]{2,1,0:T(8,128)(2,1)S(1)}, u32[]{:S(2)}, u32[]{:S(2)}) async-start(bf16[32,160,128]{2,1,0:T(8,128)(2,1)} %shard_map.66), calls=%async_computation.7 | async-start | bytes 2621440 | tf_op jit(solution)/shard_map/all_to_all | solution.py:235
  214.4 2.2 copy-start.4
  219.3 9.0 %collective-permute-start.6 = (bf16[512,512]{1,0:T(8,128)(2,1)S(1)}, bf16[512,512]{1,0:T(8,128)(2,1)}, u32[]{:S(2)}, u32[]{:S(2)}) collective-permute-start(bf16[512,512]{1,0:T(8,128)(2,1)S(1)} %shard_map.72), channel_id=1, source_target_pairs={{0,2},{2,0},{1,3},{3,1},{4,6},{6,4},{5,7},{7,5},{8,10},{10,8},{9,1... | collective-permute-start | bytes 1572872 | tf_op jit(solution)/shard_map/ppermute | solution.py:329
  222.8 16.2 %collective-permute-start.2 = (bf16[512,512]{1,0:T(8,128)(2,1)}, bf16[512,512]{1,0:T(8,128)(2,1)S(1)}, u32[]{:S(2)}, u32[]{:S(2)}) collective-permute-start(bf16[512,512]{1,0:T(8,128)(2,1)} %shard_map.68), channel_id=1, source_target_pairs={{0,2},{2,0},{1,3},{3,1},{4,6},{6,4},{5,7},{7,5},{8,10},{10,8},{9,1... | collective-permute-start | bytes 1572872 | tf_op jit(solution)/shard_map/ppermute | solution.py:329
  223.2 2.2 copy-start.5
  225.4 2.8 %copy-start.20 = (bf16[1152,512]{1,0:T(8,128)(2,1)S(1)}, bf16[1152,512]{1,0:T(8,128)(2,1)}, u32[]{:S(2)}) copy-start(bf16[1152,512]{1,0:T(8,128)(2,1)} %copy-done.19) | copy-start | bytes 3538948
  228.3 7.9 %copy-start.6 = (bf16[2,512,2048]{2,1,0:T(8,128)(2,1)S(1)}, bf16[2,512,2048]{2,1,0:T(8,128)(2,1)}, u32[]{:S(2)}) copy-start(bf16[2,512,2048]{2,1,0:T(8,128)(2,1)} %x_ref.15) | copy-start | bytes 12582916
  231.2 12.9 %collective-permute-start.8 = (bf16[256,512]{1,0:T(8,128)(2,1)}, bf16[256,512]{1,0:T(8,128)(2,1)}, u32[]{:S(2)}, u32[]{:S(2)}) collective-permute-start(bf16[256,512]{1,0:T(8,128)(2,1)} %get-tuple-element.51), channel_id=1, source_target_pairs={{0,1},{1,0},{2,3},{3,2},{4,5},{5,4},{6,7},{7,6},{8,9},{9,8},{10,11... | collective-permute-start | bytes 786440 | tf_op jit(solution)/shard_map/ppermute | solution.py:347
  232.2 12.7 %collective-permute-start.9 = (bf16[256,512]{1,0:T(8,128)(2,1)}, bf16[256,512]{1,0:T(8,128)(2,1)}, u32[]{:S(2)}, u32[]{:S(2)}) collective-permute-start(bf16[256,512]{1,0:T(8,128)(2,1)} %get-tuple-element.52), channel_id=1, source_target_pairs={{0,3},{1,2},{2,1},{3,0},{4,7},{5,6},{6,5},{7,4},{8,11},{9,10},{10,... | collective-permute-start | bytes 786440 | tf_op jit(solution)/shard_map/ppermute | solution.py:348
  235.4 3.5 %copy-start.12 = (bf16[256,512]{1,0:T(8,128)(2,1)}, bf16[256,512]{1,0:T(8,128)(2,1)S(1)}, u32[]{:S(2)}) copy-start(bf16[256,512]{1,0:T(8,128)(2,1)S(1)} %get-tuple-element.49.a_ref) | copy-start | bytes 786436
  235.4 9.5 %collective-permute-start.7 = (bf16[256,512]{1,0:T(8,128)(2,1)}, bf16[256,512]{1,0:T(8,128)(2,1)}, u32[]{:S(2)}, u32[]{:S(2)}) collective-permute-start(bf16[256,512]{1,0:T(8,128)(2,1)} %get-tuple-element.50), channel_id=1, source_target_pairs={{0,2},{2,0},{1,3},{3,1},{4,6},{6,4},{5,7},{7,5},{8,10},{10,8},{9,1... | collective-permute-start | bytes 786440 | tf_op jit(solution)/shard_map/ppermute | solution.py:329
  238.9 1.1 copy-start.11
  241.7 3.3 %copy-start.13 = (bf16[256,512]{1,0:T(8,128)(2,1)S(1)}, bf16[256,512]{1,0:T(8,128)(2,1)}, u32[]{:S(2)}) copy-start(bf16[256,512]{1,0:T(8,128)(2,1)} %copy-done.12) | copy-start | bytes 786436
  241.7 3.2 %copy-start.14 = (f32[2048]{0:T(1024)S(1)}, f32[2048]{0:T(1024)}, u32[]{:S(2)}) copy-start(f32[2048]{0:T(1024)} %param.9) | copy-start | bytes 24580
  242.9 5.2 %collective-permute-start.3 = (bf16[256,512]{1,0:T(8,128)(2,1)S(1)}, bf16[256,512]{1,0:T(8,128)(2,1)S(1)}, u32[]{:S(2)}, u32[]{:S(2)}) collective-permute-start(bf16[256,512]{1,0:T(8,128)(2,1)S(1)} %get-tuple-element.44), channel_id=1, source_target_pairs={{0,2},{2,0},{1,3},{3,1},{4,6},{6,4},{5,7},{7,5},{8,10},{10,8},{9,1... | collective-permute-start | bytes 786440 | tf_op jit(solution)/shard_map/ppermute | solution.py:329
  243.1 9.1 %collective-permute-start.4 = (bf16[256,512]{1,0:T(8,128)(2,1)S(1)}, bf16[256,512]{1,0:T(8,128)(2,1)S(1)}, u32[]{:S(2)}, u32[]{:S(2)}) collective-permute-start(bf16[256,512]{1,0:T(8,128)(2,1)S(1)} %get-tuple-element.45), channel_id=1, source_target_pairs={{0,1},{1,0},{2,3},{3,2},{4,5},{5,4},{6,7},{7,6},{8,9},{9,8},{10,11... | collective-permute-start | bytes 786440 | tf_op jit(solution)/shard_map/ppermute | solution.py:347
  244.1 12.8 %collective-permute-start.5 = (bf16[256,512]{1,0:T(8,128)(2,1)S(1)}, bf16[256,512]{1,0:T(8,128)(2,1)S(1)}, u32[]{:S(2)}, u32[]{:S(2)}) collective-permute-start(bf16[256,512]{1,0:T(8,128)(2,1)S(1)} %get-tuple-element.46), channel_id=1, source_target_pairs={{0,3},{1,2},{2,1},{3,0},{4,7},{5,6},{6,5},{7,4},{8,11},{9,10},{10,... | collective-permute-start | bytes 786440 | tf_op jit(solution)/shard_map/ppermute | solution.py:348
